TPU v7x, 128 devices: a whole 4x4x4 slice. The times are simulated.
128 devices in a mesh: enc: 4 (over y), pool: 32 (over z, x, core).
Axes of the slice: x: 4, y: 4, z: 4, core: 2. Of those that a mesh axis runs over, the one named last changes fastest.
Arguments:
- encoded: bfloat16 [8192, 32, 128], P('pool', 'enc'), may hold values from -6 to 6
- slot_items: int32 [8192], replicated, may hold values from 0 to 8191, as said below
- lengths: int32 [8192], P(('enc', 'pool')), may hold values from 1 to 32
- token_mask: int32 [8192, 32], P(('enc', 'pool')), may hold values 0 or 1
Outputs:
- scores: float32 [8192, 192], P(('enc', 'pool'))
Inputs may be any that keep to these rules, and one draw needn't show every extreme that they name: `slot_items`: each item appears in exactly one slot. The slots d * 64 + p * 2 + j, for j below 2, hold items p * 256 to (p + 1) * 256 - 1, those whose encoder rows lie on pool index p.
All inputs are finite; a program needn't handle non-finite values. No bound on the sum of `token_mask` on one device may be relied on, other than what follows from the above.
Results may differ from a plain program's by a relative error of at most 0.00057.
Values may be sent and summed in bfloat16 or wider, within the bound.
A program may use at most 64 MiB of HBM per device.

v0:
```python
import jax
import jax.numpy as jnp
from jax import lax
from jax.sharding import PartitionSpec as P


def from_partner(array, axis, stride):
    return lax.ppermute(array, axis, [(i, i ^ 1 << stride) for i in range(lax.axis_size(axis))])


def tile_scores(block, bias, other, other_bias, tok):
    query_items = block.shape[0] // tok
    other_items = other.shape[0] // tok
    width = block.shape[1]
    rows = min(32, query_items)
    blocks = query_items // rows
    other_tr = jnp.transpose(other.reshape(other_items, tok, width), (1, 0, 2))
    other_float = other_bias.astype(jnp.float32)
    other_add_tr = jnp.transpose(other_float.reshape(other_items, tok), (1, 0))[:, :, None]
    other_owner = (jnp.arange(other_items * tok, dtype=jnp.int32) // tok)[:, None] == jnp.arange(
        other_items, dtype=jnp.int32
    )[None, :]
    other_select = jnp.where((other_bias == 0)[:, None] & other_owner, 1.0, 0.0).astype(jnp.float32)
    query_flat = block.reshape(blocks, rows * tok, width)
    query_tr = jnp.transpose(block.reshape(blocks, rows, tok, width), (0, 2, 1, 3))
    bias_float = bias.astype(jnp.float32).reshape(blocks, rows, tok)
    query_add_tr = jnp.transpose(bias_float, (0, 2, 1))[..., None]
    query_valid = (bias == 0).reshape(blocks, rows * tok)
    query_owner = (jnp.arange(rows * tok, dtype=jnp.int32) // tok)[:, None] == jnp.arange(
        rows, dtype=jnp.int32
    )[None, :]

    def one_block(operands):
        flat, turned, adding, kept = operands
        dots_fore = jnp.einsum("ubh,qh->ubq", other_tr, flat, preferred_element_type=jnp.float32)
        fore = jnp.max(dots_fore + other_add_tr, axis=0)
        select = jnp.where(kept[:, None] & query_owner, 1.0, 0.0).astype(jnp.float32)
        fore = jnp.dot(
            fore, select, precision=lax.Precision.HIGHEST, preferred_element_type=jnp.float32
        )
        dots_back = jnp.einsum("trh,ch->trc", turned, other, preferred_element_type=jnp.float32)
        back = jnp.max(dots_back + adding, axis=0)
        back = jnp.dot(
            back, other_select, precision=lax.Precision.HIGHEST, preferred_element_type=jnp.float32
        )
        return 0.5 * (fore.T + back)

    result = lax.map(one_block, (query_flat, query_tr, query_add_tr, query_valid))
    return result.reshape(query_items, other_items)


def shards(encoded, slot_items, lengths, token_mask):
    n_enc = lax.axis_size("enc")
    n_pool = lax.axis_size("pool")
    owners = n_enc * n_pool
    group = encoded.shape[0]
    toks = encoded.shape[1]
    width = encoded.shape[2]
    items_dev = lengths.shape[0]
    per = items_dev // n_pool
    pool_index = lax.axis_index("pool")
    table = slot_items.reshape(owners, n_pool, per)
    mine = lax.dynamic_index_in_dim(table, pool_index, 1, keepdims=False) - pool_index * group
    outgoing = jnp.take(encoded, mine, axis=0)
    arrived = lax.all_to_all(outgoing, ("enc", "pool"), split_axis=0, concat_axis=0, tiled=True)
    arrived = arrived.reshape(n_enc, n_pool, per, toks, width)
    tok = n_enc * toks
    slotted = jnp.transpose(arrived, (1, 2, 0, 3, 4)).reshape(items_dev, tok, width)
    values = slotted.astype(jnp.float32)
    normed = (values / jnp.sqrt(jnp.sum(values * values, axis=-1, keepdims=True) + 1e-06)).astype(
        jnp.bfloat16
    )
    position = jnp.arange(tok, dtype=jnp.int32)[None, :]
    valid = (position < lengths[:, None]) & ((position == 0) | (token_mask == 1))
    bias = jnp.where(valid, 0.0, -4.0).astype(jnp.bfloat16).reshape(-1)
    block = normed.reshape(items_dev * tok, width)
    results = []
    for bit in range(3):
        other, other_bias = from_partner((block, bias), "pool", bit)
        results.append(tile_scores(block, bias, other, other_bias, tok))
    return jnp.concatenate(results, axis=1)


def solution(mesh):
    in_specs = (P("pool", "enc", None), P(), P(("enc", "pool")), P(("enc", "pool"), None))
    out_specs = P(("enc", "pool"), None)
    return jax.shard_map(shards, mesh=mesh, in_specs=in_specs, out_specs=out_specs, check_vma=False)
```

profile of v0, /device:TPU:0, one launch (start us, length us, event | category | flops | bytes accessed | tf_op | source)
XLA Modules:
  0.0 85.1 jit_solution(14227615750113908379)
XLA Ops:
  0.0 0.9 %broadcast_compare_fusion = (pred[64,32]{0,1:T(8,128)(4,1)S(1)}, bf16[64,32]{0,1:T(8,128)(2,1)S(1)}) fusion(s32[64,32]{0,1:T(8,128)} %param.13, pred[32]{0:T(512)(128)(4,1)S(1)} %iota_compare_fusion.7, s32[64]{0:T(128)} %param.12), kind=kLoop, calls=%fused_computation.142 | loop fusion | flops 18432 | bytes 14624 | tf_op jit(solution)/shard_map/eq | solution.py:28
  1.1 3.1 %collective-permute-start.5 = (bf16[2048]{0:T(1024)(128)(2,1)S(1)}, bf16[2048]{0:T(1024)(128)(2,1)S(1)}, u32[]{:S(2)}, u32[]{:S(2)}) collective-permute-start(bf16[2048]{0:T(1024)(128)(2,1)S(1)} %reshape.171), channel_id=1, source_target_pairs={{0,4},{1,5},{2,6},{3,7},{4,0},{5,1},{6,2},{7,3},{8,12},{9,13},{10,... | collective-permute-start | bytes 12296 | tf_op jit(solution)/shard_map/ppermute | solution.py:8
  4.2 0.6 collective-permute-start.3
  4.8 2.8 %reshape.169 = s32[128,32,2]{2,1,0:T(8,128)S(1)} reshape(s32[8192]{0:T(1024)} %param.11) | data formatting | bytes 65536 | tf_op jit(solution)/shard_map/reshape | solution.py:62
  7.9 0.8 gather_fusion
  8.7 1.1 %broadcast_select_fusion = bf16[128,2,8,128]{3,2,1,0:T(8,128)(2,1)} fusion(bf16[128,2,8,128]{3,2,1,0:T(8,128)(2,1)S(1)} %bitcast.165, pred[128,2]{1,0:T(8,128)(4,1)S(1)} %compare_and_fusion), kind=kLoop, calls=%fused_computation.118 | loop fusion | flops 262144 | bytes 1048832 | tf_op jit(solution)/shard_map/jit(_take)/select_n | solution.py:64
  9.9 10.2 %all-to-all-start = ((bf16[128,2,8,128]{3,2,1,0:T(8,128)(2,1)}), bf16[128,2,8,128]{3,2,1,0:T(8,128)(2,1)S(1)}, u32[]{:S(2)}, u32[]{:S(2)}) async-start(bf16[128,2,8,128]{3,2,1,0:T(8,128)(2,1)} %broadcast_select_fusion), calls=%async_computation | async-start | bytes 1048576 | tf_op jit(solution)/shard_map/all_to_all | solution.py:65
  20.9 12.7 %all-to-all-done = bf16[128,2,8,128]{3,2,1,0:T(8,128)(2,1)S(1)} async-done(((bf16[128,2,8,128]{3,2,1,0:T(8,128)(2,1)}), bf16[128,2,8,128]{3,2,1,0:T(8,128)(2,1)S(1)}, u32[]{:S(2)}, u32[]{:S(2)}) %all-to-all-start) | async-done | bytes 524320 | tf_op jit(solution)/shard_map/all_to_all | solution.py:65
  33.6 0.4 multiply_reduce_fusion
  34.5 0.2 sqrt.20
  35.0 0.3 fusion.99
  35.4 0.9 %collective-permute-start.4 = (bf16[2048,128]{1,0:T(8,128)(2,1)S(1)}, bf16[2048,128]{1,0:T(8,128)(2,1)S(1)}, u32[]{:S(2)}, u32[]{:S(2)}) collective-permute-start(bf16[2048,128]{1,0:T(8,128)(2,1)S(1)} %fusion.99), channel_id=1, source_target_pairs={{0,4},{1,5},{2,6},{3,7},{4,0},{5,1},{6,2},{7,3},{8,12},{9,13},{10,... | collective-permute-start | bytes 1572872 | tf_op jit(solution)/shard_map/ppermute | solution.py:8
  36.3 0.8 collective-permute-start.2
  37.0 0.3 fusion.100
  37.4 0.2 copy.79
  37.6 0.3 divide_convert_fusion.1
  38.0 13.8 %collective-permute-done.4 = bf16[2048,128]{1,0:T(8,128)(2,1)S(1)} collective-permute-done((bf16[2048,128]{1,0:T(8,128)(2,1)S(1)}, bf16[2048,128]{1,0:T(8,128)(2,1)S(1)}, u32[]{:S(2)}, u32[]{:S(2)}) %collective-permute-start.4) | collective-permute-done | bytes 524320 | tf_op jit(solution)/shard_map/ppermute | solution.py:8
  51.8 1.0 %copy.92 = bf16[64,32,128]{2,0,1:T(8,128)(2,1)} copy(bf16[64,32,128]{2,1,0:T(8,128)(2,1)S(1)} %bitcast.170) | data formatting | bytes 1048576 | tf_op jit(solution)/shard_map/reshape | solution.py:17
  52.8 11.5 %while.35 = (s32[]{:T(128)}, f32[2,32,64]{2,1,0:T(8,128)S(1)}, pred[2,1024]{1,0:T(4,128)(4,1)S(1)}, bf16[2,1024,128]{2,1,0:T(8,128)(2,1)S(1)}, bf16[32,64,128]{2...) while((s32[]{:T(128)}, f32[2,32,64]{2,1,0:T(8,128)S(1)}, ...), condition=%wide.region_12.13_spmd.clone, body=%wide.region_9.12_spmd.clone.sunk | while | flops 1157992448 | bytes 4818101 | solution.py:48
  52.8 2.4 %add_reduce_fusion.17 = f32[32,2048]{1,0:T(8,128)S(1)} fusion(f32[32,32]{1,0:T(8,128)S(1)} %dynamic-slice_bitcast_fusion.8, bf16[2048,128]{1,0:T(8,128)(2,1)} %get-tuple-element.739, bf16[2,32,32,128]{3,2,1,0:T(8,128)(2,1)S(1)} %get-tuple-element.738, s32[]{:T(128)S(6)} %copy.100), kind=kOutput, calls=%fused_computation.75.clone.1 | convolution fusion | flops 540999680 | bytes 1064964 | tf_op jit(solution)/shard_map/while/body/eval_jaxpr/trh,ch->trc/dot_general | solution.py:41
  55.2 1.3 %add_reduce_fusion.16 = f32[1024,64]{0,1:T(8,128)S(1)} fusion(f32[32,64]{1,0:T(8,128)S(1)} %bitcast.184, bf16[32,64,128]{2,1,0:T(8,128)(2,1)S(1)} %copy-done.2, bf16[2,1024,128]{2,1,0:T(8,128)(2,1)S(1)} %get-tuple-element.735, s32[]{:T(128)S(6)} %copy.100), kind=kOutput, calls=%fused_computation.76.clone.1 | convolution fusion | flops 540999680 | bytes 1064964 | tf_op jit(solution)/shard_map/while/body/eval_jaxpr/ubh,qh->ubq/dot_general | solution.py:35
  56.5 0.9 %fusion.175 = f32[32,64]{1,0:T(8,128)S(1)} fusion(f32[1024,64]{0,1:T(8,128)S(1)} %add_reduce_fusion.16, s32[1024]{0:T(1024)S(1)} %get-tuple-element.741, pred[1024]{0:T(1024)(128)(4,1)S(1)} %dynamic-slice_reduce_fusion.8), kind=kOutput, calls=%fused_computation.89.clone.1 | convolution fusion | flops 25264128 | bytes 275456 | tf_op jit(solution)/shard_map/while/body/eval_jaxpr/dot_general | solution.py:38
  57.5 1.1 %fusion.176 = f32[2,32,64]{2,1,0:T(8,128)S(1)} fusion(f32[2,32,64]{2,1,0:T(8,128)S(1)} %get-tuple-element.720, s32[]{:T(128)S(6)} %copy.100, f32[32,64]{1,0:T(8,128)S(1)} %fusion.175, f32[32,2048]{1,0:T(8,128)S(1)} %add_reduce_fusion.17, s32[2048]{0:T(1024)S(1)} %get-tuple-element.742, pred[2048]{0:T(1024)(128)(4,1)S(1)} %get-tuple-element.743), kind=kOutput, calls=%fused_computation.80.clone.1 | convolution fusion | flops 50728960 | bytes 305156 | tf_op jit(solution)/shard_map/while/body/eval_jaxpr/dot_general | solution.py:43
  58.6 2.4 %add_reduce_fusion.17 = f32[32,2048]{1,0:T(8,128)S(1)} fusion(f32[32,32]{1,0:T(8,128)S(1)} %dynamic-slice_bitcast_fusion.8, bf16[2048,128]{1,0:T(8,128)(2,1)} %get-tuple-element.739, bf16[2,32,32,128]{3,2,1,0:T(8,128)(2,1)S(1)} %get-tuple-element.738, s32[]{:T(128)S(6)} %copy.100), kind=kOutput, calls=%fused_computation.75.clone.1 | convolution fusion | flops 540999680 | bytes 1064964 | tf_op jit(solution)/shard_map/while/body/eval_jaxpr/trh,ch->trc/dot_general | solution.py:41
  61.0 1.3 %add_reduce_fusion.16 = f32[1024,64]{0,1:T(8,128)S(1)} fusion(f32[32,64]{1,0:T(8,128)S(1)} %bitcast.184, bf16[32,64,128]{2,1,0:T(8,128)(2,1)S(1)} %copy-done.2, bf16[2,1024,128]{2,1,0:T(8,128)(2,1)S(1)} %get-tuple-element.735, s32[]{:T(128)S(6)} %copy.100), kind=kOutput, calls=%fused_computation.76.clone.1 | convolution fusion | flops 540999680 | bytes 1064964 | tf_op jit(solution)/shard_map/while/body/eval_jaxpr/ubh,qh->ubq/dot_general | solution.py:35
  62.3 0.9 %fusion.175 = f32[32,64]{1,0:T(8,128)S(1)} fusion(f32[1024,64]{0,1:T(8,128)S(1)} %add_reduce_fusion.16, s32[1024]{0:T(1024)S(1)} %get-tuple-element.741, pred[1024]{0:T(1024)(128)(4,1)S(1)} %dynamic-slice_reduce_fusion.8), kind=kOutput, calls=%fused_computation.89.clone.1 | convolution fusion | flops 25264128 | bytes 275456 | tf_op jit(solution)/shard_map/while/body/eval_jaxpr/dot_general | solution.py:38
  63.2 1.1 %fusion.176 = f32[2,32,64]{2,1,0:T(8,128)S(1)} fusion(f32[2,32,64]{2,1,0:T(8,128)S(1)} %get-tuple-element.720, s32[]{:T(128)S(6)} %copy.100, f32[32,64]{1,0:T(8,128)S(1)} %fusion.175, f32[32,2048]{1,0:T(8,128)S(1)} %add_reduce_fusion.17, s32[2048]{0:T(1024)S(1)} %get-tuple-element.742, pred[2048]{0:T(1024)(128)(4,1)S(1)} %get-tuple-element.743), kind=kOutput, calls=%fused_computation.80.clone.1 | convolution fusion | flops 50728960 | bytes 305156 | tf_op jit(solution)/shard_map/while/body/eval_jaxpr/dot_general | solution.py:43
  64.3 1.0 %copy.93 = bf16[64,32,128]{2,0,1:T(8,128)(2,1)} copy(bf16[64,32,128]{2,1,0:T(8,128)(2,1)S(1)} %bitcast.169) | data formatting | bytes 1048576 | tf_op jit(solution)/shard_map/reshape | solution.py:17
  65.3 9.3 %while.34 = (s32[]{:T(128)}, f32[2,32,64]{2,1,0:T(8,128)S(1)}, pred[2,1024]{1,0:T(4,128)(4,1)S(1)}, bf16[2,1024,128]{2,1,0:T(8,128)(2,1)S(1)}, bf16[32,64,128]{2...) while((s32[]{:T(128)}, f32[2,32,64]{2,1,0:T(8,128)S(1)}, ...), condition=%wide.region_8.9_spmd.clone, body=%wide.region_5.8_spmd.clone.sunk | while | flops 1157992448 | bytes 4818101 | solution.py:48
  65.4 1.3 %add_reduce_fusion.15 = f32[32,2048]{1,0:T(8,128)S(1)} fusion(f32[32,32]{1,0:T(8,128)S(1)} %dynamic-slice_bitcast_fusion.7, bf16[2048,128]{1,0:T(8,128)(2,1)S(1)} %get-tuple-element.778, bf16[2,32,32,128]{3,2,1,0:T(8,128)(2,1)S(1)} %get-tuple-element.777, s32[]{:T(128)S(6)} %copy.106), kind=kOutput, calls=%fused_computation.41.clone.1 | convolution fusion | flops 540999680 | bytes 1064964 | tf_op jit(solution)/shard_map/while/body/eval_jaxpr/trh,ch->trc/dot_general | solution.py:41
  66.7 1.3 %add_reduce_fusion.14 = f32[1024,64]{0,1:T(8,128)S(1)} fusion(f32[32,64]{1,0:T(8,128)S(1)} %bitcast.183, bf16[32,64,128]{2,1,0:T(8,128)(2,1)S(1)} %copy-done.3, bf16[2,1024,128]{2,1,0:T(8,128)(2,1)S(1)} %get-tuple-element.774, s32[]{:T(128)S(6)} %copy.106), kind=kOutput, calls=%fused_computation.42.clone.1 | convolution fusion | flops 540999680 | bytes 1064964 | tf_op jit(solution)/shard_map/while/body/eval_jaxpr/ubh,qh->ubq/dot_general | solution.py:35
  68.0 0.9 %fusion.165 = f32[32,64]{1,0:T(8,128)S(1)} fusion(f32[1024,64]{0,1:T(8,128)S(1)} %add_reduce_fusion.14, s32[1024]{0:T(1024)S(1)} %get-tuple-element.780, pred[1024]{0:T(1024)(128)(4,1)S(1)} %dynamic-slice_reduce_fusion.7), kind=kOutput, calls=%fused_computation.55.clone.1 | convolution fusion | flops 25264128 | bytes 275456 | tf_op jit(solution)/shard_map/while/body/eval_jaxpr/dot_general | solution.py:38
  68.9 1.1 %fusion.166 = f32[2,32,64]{2,1,0:T(8,128)S(1)} fusion(f32[2,32,64]{2,1,0:T(8,128)S(1)} %get-tuple-element.759, s32[]{:T(128)S(6)} %copy.106, f32[32,64]{1,0:T(8,128)S(1)} %fusion.165, f32[32,2048]{1,0:T(8,128)S(1)} %add_reduce_fusion.15, s32[2048]{0:T(1024)S(1)} %get-tuple-element.781, pred[2048]{0:T(1024)(128)(4,1)S(1)} %get-tuple-element.782), kind=kOutput, calls=%fused_computation.46.clone.1 | convolution fusion | flops 50728960 | bytes 305156 | tf_op jit(solution)/shard_map/while/body/eval_jaxpr/dot_general | solution.py:43
  70.0 1.3 %add_reduce_fusion.15 = f32[32,2048]{1,0:T(8,128)S(1)} fusion(f32[32,32]{1,0:T(8,128)S(1)} %dynamic-slice_bitcast_fusion.7, bf16[2048,128]{1,0:T(8,128)(2,1)S(1)} %get-tuple-element.778, bf16[2,32,32,128]{3,2,1,0:T(8,128)(2,1)S(1)} %get-tuple-element.777, s32[]{:T(128)S(6)} %copy.106), kind=kOutput, calls=%fused_computation.41.clone.1 | convolution fusion | flops 540999680 | bytes 1064964 | tf_op jit(solution)/shard_map/while/body/eval_jaxpr/trh,ch->trc/dot_general | solution.py:41
  71.3 1.3 %add_reduce_fusion.14 = f32[1024,64]{0,1:T(8,128)S(1)} fusion(f32[32,64]{1,0:T(8,128)S(1)} %bitcast.183, bf16[32,64,128]{2,1,0:T(8,128)(2,1)S(1)} %copy-done.3, bf16[2,1024,128]{2,1,0:T(8,128)(2,1)S(1)} %get-tuple-element.774, s32[]{:T(128)S(6)} %copy.106), kind=kOutput, calls=%fused_computation.42.clone.1 | convolution fusion | flops 540999680 | bytes 1064964 | tf_op jit(solution)/shard_map/while/body/eval_jaxpr/ubh,qh->ubq/dot_general | solution.py:35
  72.6 0.9 %fusion.165 = f32[32,64]{1,0:T(8,128)S(1)} fusion(f32[1024,64]{0,1:T(8,128)S(1)} %add_reduce_fusion.14, s32[1024]{0:T(1024)S(1)} %get-tuple-element.780, pred[1024]{0:T(1024)(128)(4,1)S(1)} %dynamic-slice_reduce_fusion.7), kind=kOutput, calls=%fused_computation.55.clone.1 | convolution fusion | flops 25264128 | bytes 275456 | tf_op jit(solution)/shard_map/while/body/eval_jaxpr/dot_general | solution.py:38
  73.6 1.1 %fusion.166 = f32[2,32,64]{2,1,0:T(8,128)S(1)} fusion(f32[2,32,64]{2,1,0:T(8,128)S(1)} %get-tuple-element.759, s32[]{:T(128)S(6)} %copy.106, f32[32,64]{1,0:T(8,128)S(1)} %fusion.165, f32[32,2048]{1,0:T(8,128)S(1)} %add_reduce_fusion.15, s32[2048]{0:T(1024)S(1)} %get-tuple-element.781, pred[2048]{0:T(1024)(128)(4,1)S(1)} %get-tuple-element.782), kind=kOutput, calls=%fused_computation.46.clone.1 | convolution fusion | flops 50728960 | bytes 305156 | tf_op jit(solution)/shard_map/while/body/eval_jaxpr/dot_general | solution.py:43
  74.7 0.2 copy.94
  74.9 9.5 %while.33 = (s32[]{:T(128)}, f32[2,32,64]{2,1,0:T(8,128)S(1)}, pred[2,1024]{1,0:T(4,128)(4,1)S(1)}, bf16[2,1024,128]{2,1,0:T(8,128)(2,1)S(1)}, bf16[32,64,128]{2...) while((s32[]{:T(128)}, f32[2,32,64]{2,1,0:T(8,128)S(1)}, ...), condition=%wide.region_4.5_spmd.clone, body=%wide.region_1.4_spmd.clone.sunk | while | flops 1157992448 | bytes 2720921 | solution.py:48
  75.2 1.3 %add_reduce_fusion.13 = f32[32,2048]{1,0:T(8,128)S(1)} fusion(f32[32,32]{1,0:T(8,128)S(1)} %dynamic-slice_bitcast_fusion.6, bf16[2048,128]{1,0:T(8,128)(2,1)S(1)} %get-tuple-element.817, bf16[2,32,32,128]{3,2,1,0:T(8,128)(2,1)S(1)} %get-tuple-element.816, s32[]{:T(128)S(6)} %copy.112), kind=kOutput, calls=%fused_computation.7.clone.1 | convolution fusion | flops 540999680 | bytes 1064964 | tf_op jit(solution)/shard_map/while/body/eval_jaxpr/trh,ch->trc/dot_general | solution.py:41
  76.5 1.3 %add_reduce_fusion.12 = f32[1024,64]{0,1:T(8,128)S(1)} fusion(f32[32,64]{1,0:T(8,128)S(1)} %bitcast.182, bf16[32,64,128]{2,1,0:T(8,128)(2,1)S(1)} %get-tuple-element.814, bf16[2,1024,128]{2,1,0:T(8,128)(2,1)S(1)} %get-tuple-element.813, s32[]{:T(128)S(6)} %copy.112), kind=kOutput, calls=%fused_computation.8.clone.1 | convolution fusion | flops 540999680 | bytes 1064964 | tf_op jit(solution)/shard_map/while/body/eval_jaxpr/ubh,qh->ubq/dot_general | solution.py:35
  77.7 0.9 %fusion.155 = f32[32,64]{1,0:T(8,128)S(1)} fusion(f32[1024,64]{0,1:T(8,128)S(1)} %add_reduce_fusion.12, s32[1024]{0:T(1024)S(1)} %get-tuple-element.819, pred[1024]{0:T(1024)(128)(4,1)S(1)} %dynamic-slice_reduce_fusion.6), kind=kOutput, calls=%fused_computation.21.clone.1 | convolution fusion | flops 25264128 | bytes 275456 | tf_op jit(solution)/shard_map/while/body/eval_jaxpr/dot_general | solution.py:38
  78.7 1.1 %fusion.156 = f32[2,32,64]{2,1,0:T(8,128)S(1)} fusion(f32[2,32,64]{2,1,0:T(8,128)S(1)} %get-tuple-element.798, s32[]{:T(128)S(6)} %copy.112, f32[32,64]{1,0:T(8,128)S(1)} %fusion.155, f32[32,2048]{1,0:T(8,128)S(1)} %add_reduce_fusion.13, s32[2048]{0:T(1024)S(1)} %get-tuple-element.820, pred[2048]{0:T(1024)(128)(4,1)S(1)} %get-tuple-element.821), kind=kOutput, calls=%fused_computation.12.clone.1 | convolution fusion | flops 50728960 | bytes 305156 | tf_op jit(solution)/shard_map/while/body/eval_jaxpr/dot_general | solution.py:43
  79.8 1.3 %add_reduce_fusion.13 = f32[32,2048]{1,0:T(8,128)S(1)} fusion(f32[32,32]{1,0:T(8,128)S(1)} %dynamic-slice_bitcast_fusion.6, bf16[2048,128]{1,0:T(8,128)(2,1)S(1)} %get-tuple-element.817, bf16[2,32,32,128]{3,2,1,0:T(8,128)(2,1)S(1)} %get-tuple-element.816, s32[]{:T(128)S(6)} %copy.112), kind=kOutput, calls=%fused_computation.7.clone.1 | convolution fusion | flops 540999680 | bytes 1064964 | tf_op jit(solution)/shard_map/while/body/eval_jaxpr/trh,ch->trc/dot_general | solution.py:41
  81.1 1.3 %add_reduce_fusion.12 = f32[1024,64]{0,1:T(8,128)S(1)} fusion(f32[32,64]{1,0:T(8,128)S(1)} %bitcast.182, bf16[32,64,128]{2,1,0:T(8,128)(2,1)S(1)} %get-tuple-element.814, bf16[2,1024,128]{2,1,0:T(8,128)(2,1)S(1)} %get-tuple-element.813, s32[]{:T(128)S(6)} %copy.112), kind=kOutput, calls=%fused_computation.8.clone.1 | convolution fusion | flops 540999680 | bytes 1064964 | tf_op jit(solution)/shard_map/while/body/eval_jaxpr/ubh,qh->ubq/dot_general | solution.py:35
  82.4 0.9 %fusion.155 = f32[32,64]{1,0:T(8,128)S(1)} fusion(f32[1024,64]{0,1:T(8,128)S(1)} %add_reduce_fusion.12, s32[1024]{0:T(1024)S(1)} %get-tuple-element.819, pred[1024]{0:T(1024)(128)(4,1)S(1)} %dynamic-slice_reduce_fusion.6), kind=kOutput, calls=%fused_computation.21.clone.1 | convolution fusion | flops 25264128 | bytes 275456 | tf_op jit(solution)/shard_map/while/body/eval_jaxpr/dot_general | solution.py:38
  83.3 1.1 %fusion.156 = f32[2,32,64]{2,1,0:T(8,128)S(1)} fusion(f32[2,32,64]{2,1,0:T(8,128)S(1)} %get-tuple-element.798, s32[]{:T(128)S(6)} %copy.112, f32[32,64]{1,0:T(8,128)S(1)} %fusion.155, f32[32,2048]{1,0:T(8,128)S(1)} %add_reduce_fusion.13, s32[2048]{0:T(1024)S(1)} %get-tuple-element.820, pred[2048]{0:T(1024)(128)(4,1)S(1)} %get-tuple-element.821), kind=kOutput, calls=%fused_computation.12.clone.1 | convolution fusion | flops 50728960 | bytes 305156 | tf_op jit(solution)/shard_map/while/body/eval_jaxpr/dot_general | solution.py:43
  84.4 0.7 pad_maximum_fusion
  (65 shorter events, 2.2 us)
Async XLA Ops:
  0.0 7.9 %copy-start = (bf16[256,8,128]{2,1,0:T(8,128)(2,1)S(1)}, bf16[256,8,128]{2,1,0:T(8,128)(2,1)}, u32[]{:S(2)}) copy-start(bf16[256,8,128]{2,1,0:T(8,128)(2,1)} %param.10) | copy-start | bytes 1572868
  1.1 19.3 %collective-permute-start.5 = (bf16[2048]{0:T(1024)(128)(2,1)S(1)}, bf16[2048]{0:T(1024)(128)(2,1)S(1)}, u32[]{:S(2)}, u32[]{:S(2)}) collective-permute-start(bf16[2048]{0:T(1024)(128)(2,1)S(1)} %reshape.171), channel_id=1, source_target_pairs={{0,4},{1,5},{2,6},{3,7},{4,0},{5,1},{6,2},{7,3},{8,12},{9,13},{10,... | collective-permute-start | bytes 12296 | tf_op jit(solution)/shard_map/ppermute | solution.py:8
  4.2 16.4 %collective-permute-start.3 = (bf16[2048]{0:T(1024)(128)(2,1)S(1)}, bf16[2048]{0:T(1024)(128)(2,1)S(1)}, u32[]{:S(2)}, u32[]{:S(2)}) collective-permute-start(bf16[2048]{0:T(1024)(128)(2,1)S(1)} %reshape.171), channel_id=1, source_target_pairs={{0,2},{1,3},{2,0},{3,1},{4,6},{5,7},{6,4},{7,5},{8,10},{9,11},{10,... | collective-permute-start | bytes 12296 | tf_op jit(solution)/shard_map/ppermute | solution.py:8
  4.8 15.6 %collective-permute-start.1 = (bf16[2048]{0:T(1024)(128)(2,1)S(1)}, bf16[2048]{0:T(1024)(128)(2,1)S(1)}, u32[]{:S(2)}, u32[]{:S(2)}) collective-permute-start(bf16[2048]{0:T(1024)(128)(2,1)S(1)} %reshape.171), channel_id=1, source_target_pairs={{0,1},{1,0},{2,3},{3,2},{4,5},{5,4},{6,7},{7,6},{8,9},{9,8},{10,11... | collective-permute-start | bytes 12296 | tf_op jit(solution)/shard_map/ppermute | solution.py:8
  9.9 23.7 %all-to-all-start = ((bf16[128,2,8,128]{3,2,1,0:T(8,128)(2,1)}), bf16[128,2,8,128]{3,2,1,0:T(8,128)(2,1)S(1)}, u32[]{:S(2)}, u32[]{:S(2)}) async-start(bf16[128,2,8,128]{3,2,1,0:T(8,128)(2,1)} %broadcast_select_fusion), calls=%async_computation | async-start | bytes 1048576 | tf_op jit(solution)/shard_map/all_to_all | solution.py:65
  35.4 16.4 %collective-permute-start.4 = (bf16[2048,128]{1,0:T(8,128)(2,1)S(1)}, bf16[2048,128]{1,0:T(8,128)(2,1)S(1)}, u32[]{:S(2)}, u32[]{:S(2)}) collective-permute-start(bf16[2048,128]{1,0:T(8,128)(2,1)S(1)} %fusion.99), channel_id=1, source_target_pairs={{0,4},{1,5},{2,6},{3,7},{4,0},{5,1},{6,2},{7,3},{8,12},{9,13},{10,... | collective-permute-start | bytes 1572872 | tf_op jit(solution)/shard_map/ppermute | solution.py:8
  36.3 28.1 %collective-permute-start.2 = (bf16[2048,128]{1,0:T(8,128)(2,1)S(1)}, bf16[2048,128]{1,0:T(8,128)(2,1)S(1)}, u32[]{:S(2)}, u32[]{:S(2)}) collective-permute-start(bf16[2048,128]{1,0:T(8,128)(2,1)S(1)} %fusion.99), channel_id=1, source_target_pairs={{0,2},{1,3},{2,0},{3,1},{4,6},{5,7},{6,4},{7,5},{8,10},{9,11},{10,... | collective-permute-start | bytes 1572872 | tf_op jit(solution)/shard_map/ppermute | solution.py:8
  37.0 37.6 %collective-permute-start = (bf16[2048,128]{1,0:T(8,128)(2,1)S(1)}, bf16[2048,128]{1,0:T(8,128)(2,1)S(1)}, u32[]{:S(2)}, u32[]{:S(2)}) collective-permute-start(bf16[2048,128]{1,0:T(8,128)(2,1)S(1)} %fusion.99), channel_id=1, source_target_pairs={{0,1},{1,0},{2,3},{3,2},{4,5},{5,4},{6,7},{7,6},{8,9},{9,8},{10,11... | collective-permute-start | bytes 1572872 | tf_op jit(solution)/shard_map/ppermute | solution.py:8
  51.8 1.0 %copy-start.1 = (bf16[2048,128]{1,0:T(8,128)(2,1)}, bf16[2048,128]{1,0:T(8,128)(2,1)S(1)}, u32[]{:S(2)}) copy-start(bf16[2048,128]{1,0:T(8,128)(2,1)S(1)} %collective-permute-done.4) | copy-start | bytes 1572868
  52.8 2.4 %copy-start.2 = (bf16[32,64,128]{2,1,0:T(8,128)(2,1)S(1)}, bf16[32,64,128]{2,1,0:T(8,128)(2,1)}, u32[]{:S(2)}) copy-start(bf16[32,64,128]{2,1,0:T(8,128)(2,1)} %get-tuple-element.736) | copy-start | bytes 1572868 | tf_op jit(solution)/shard_map/while
  58.6 2.4 %copy-start.2 = (bf16[32,64,128]{2,1,0:T(8,128)(2,1)S(1)}, bf16[32,64,128]{2,1,0:T(8,128)(2,1)}, u32[]{:S(2)}) copy-start(bf16[32,64,128]{2,1,0:T(8,128)(2,1)} %get-tuple-element.736) | copy-start | bytes 1572868 | tf_op jit(solution)/shard_map/while
  65.4 1.3 %copy-start.3 = (bf16[32,64,128]{2,1,0:T(8,128)(2,1)S(1)}, bf16[32,64,128]{2,1,0:T(8,128)(2,1)}, u32[]{:S(2)}) copy-start(bf16[32,64,128]{2,1,0:T(8,128)(2,1)} %get-tuple-element.775) | copy-start | bytes 1572868 | tf_op jit(solution)/shard_map/while
  70.0 1.3 %copy-start.3 = (bf16[32,64,128]{2,1,0:T(8,128)(2,1)S(1)}, bf16[32,64,128]{2,1,0:T(8,128)(2,1)}, u32[]{:S(2)}) copy-start(bf16[32,64,128]{2,1,0:T(8,128)(2,1)} %get-tuple-element.775) | copy-start | bytes 1572868 | tf_op jit(solution)/shard_map/while
where the time goes:
time: 85.4 us; the launch traced here: 85.1 us
  matrix products  29.5 us (35%)
  waiting for transfers between devices  26.5 us (31%)
  starting transfers between devices  15.6 us (18%)
  local copies, waits for them, and re-layouts  8.2 us (10%)
  other arithmetic  4.43 us (5%)
    ppermute x6, waiting for transfers between devices, from_partner(): lax.ppermute(array, axis, [(i, i ^ 1 << stride) for i in range(lax.axis_s...  13.8 us
    all_to_all x1, waiting for transfers between devices, shards(): lax.all_to_all(outgoing, ('enc', 'pool'), split_axis=0, concat_axis=0, ti...  12.7 us
    all_to_all x1, starting transfers between devices, shards(): lax.all_to_all(outgoing, ('enc', 'pool'), split_axis=0, concat_axis=0, ti...  10.2 us
    dot_general x6, matrix products, one_block(): jnp.einsum('trh,ch->trc', turned, other, preferred_element_type=jnp.float32)  9.88 us
    dot_general x6, matrix products, one_block(): jnp.einsum('ubh,qh->ubq', other_tr, flat, preferred_element_type=jnp.floa...  7.66 us
    dot_general x6, matrix products, one_block(): jnp.dot(back, other_select, precision=lax.Precision.HIGHEST, preferred_el...  6.46 us
    dot_general x6, matrix products, one_block(): jnp.dot(fore, select, precision=lax.Precision.HIGHEST, preferred_element_...  5.54 us
    ppermute x6, starting transfers between devices, from_partner(): lax.ppermute(array, axis, [(i, i ^ 1 << stride) for i in range(lax.axis_s...  5.41 us
  transfers between devices with their start and end apart: 7, of which 2 were waited for; matrix products, arithmetic and copies ran while one was open for 34% of the time, Pallas kernels for 0%

commit v1 on v0

v1 whole, which is shorter than its diff:
```python
import functools

import jax
import jax.numpy as jnp
from jax import lax
from jax.experimental import pallas as pl
from jax.experimental.pallas import tpu as pltpu
from jax.sharding import PartitionSpec as P

MESH = pl.DeviceIdType.MESH
NT = (((1,), (1,)), ((), ()))
F32 = jnp.float32
BF16 = jnp.bfloat16


def next_x(x):
    return (2 * x + 1) % 5


def prev_x(x):
    return (3 * x + 2) % 5


def spread(valid, wide):
    for t in range(32):
        wide[t] = jnp.broadcast_to(valid[:, t : t + 1], (64, 128))


def assemble(tiles, wide, out, move, first):
    for a in range(4):
        base = tiles[a * 8 : a * 8 + 8].reshape(128, 128)
        for e in range(4):
            rows = tiles[e * 32 + a * 8 : e * 32 + a * 8 + 8].reshape(128, 128)
            keep = wide[e * 8 : e * 8 + 8, a * 16 : a * 16 + 16, :].reshape(128, 128)
            take = jnp.concatenate([keep * move, (1.0 - keep) * first], axis=1).astype(BF16)
            both = jnp.concatenate([rows, base], axis=0)
            made = jnp.dot(take, both, preferred_element_type=F32).astype(BF16)
            out[e * 8 : e * 8 + 8, a * 16 : a * 16 + 16, :] = made.reshape(8, 16, 128)


def fore_sum(fore, wide, a):
    best = jnp.maximum(fore, pltpu.roll(fore, 64, 1)).reshape(32, 16, 128)
    return jnp.sum(best * wide[:, a * 16 : a * 16 + 16, :], axis=0)


def forward_only(block, other, wide, out):
    for a in range(4):
        left = block[:, a * 16 : a * 16 + 16, :].reshape(512, 128)
        fore = None
        for n in range(8):
            right = other[n * 4 : n * 4 + 4].reshape(256, 128)
            dots = lax.dot_general(left, right, NT, preferred_element_type=F32)
            part = jnp.maximum(dots[:, :128], dots[:, 128:])
            fore = part if fore is None else jnp.maximum(fore, part)
        out[a * 16 : a * 16 + 16, :] = fore_sum(fore, wide, a)


def both_ways(block, other, wide, weight, out):
    for a in range(4):
        left = block[:, a * 16 : a * 16 + 16, :].reshape(512, 128)
        fore = None
        back = None
        for n in range(8):
            right = other[n * 4 : n * 4 + 4].reshape(256, 128)
            dots = lax.dot_general(left, right, NT, preferred_element_type=F32)
            part = jnp.maximum(dots[:, :128], dots[:, 128:])
            fore = part if fore is None else jnp.maximum(fore, part)
            most = jnp.max(dots.reshape(32, 16, 256), axis=0)
            part = most[:, :128] * weight[2 * n : 2 * n + 1, :] + most[:, 128:] * weight[2 * n + 1 : 2 * n + 2, :]
            back = part if back is None else back + part
        back = back + pltpu.roll(back, 64, 1)
        out[a * 16 : a * 16 + 16, :] = 0.5 * (fore_sum(fore, wide, a) + back)


def kernel(
    x_hbm, slots_hbm, lengths_ref, mask_ref, out_ref,
    x, slots, send, tiles_own, tiles_next, block, block_next, block_core,
    valid_own, valid_next, turned, wide, wide_next,
    fore_own, fore_core, score, score_t, score_in,
    load_sem, send_own, send_next, recv_own, recv_next, sem_valid, sem_block, sem_fore, sem_score,
):
    e = lax.axis_index("enc")
    p = lax.axis_index("pool")
    z = p // 8
    xx = (p // 2) % 4
    core = p % 2
    me = e * 32 + p
    nxt = z * 8 + next_x(xx) * 2 + core
    prv = z * 8 + prev_x(xx) * 2 + core
    mate = z * 8 + xx * 2 + (1 - core)

    load_x = pltpu.make_async_copy(x_hbm, x, load_sem.at[0])
    load_slots = pltpu.make_async_copy(slots_hbm, slots, load_sem.at[1])
    load_x.start()
    load_slots.start()

    def peer(i):
        dx = (i // 2) % 4
        dz = (i // 8) % 4
        dy = i // 32
        te = (e + dy) % 4
        tz = (z + dz) % 4
        tx = (xx + dx) % 4
        tc = (core + i) % 2
        return te, tz, tx, tc

    barrier = pltpu.get_barrier_semaphore()

    def greet(i, carry):
        te, tz, tx, tc = peer(128 - i)
        pl.semaphore_signal(barrier, inc=1, device_id=(te, tz * 8 + tx * 2 + tc), device_id_type=MESH)
        return carry

    lax.fori_loop(1, 128, greet, 0)

    length = lengths_ref[...]
    row = lax.broadcasted_iota(jnp.int32, (64, 64), 0)
    col = lax.broadcasted_iota(jnp.int32, (64, 64), 1)
    length_col = jnp.sum(jnp.where(row == col, jnp.broadcast_to(length, (64, 64)), 0), axis=1, keepdims=True)
    position = lax.broadcasted_iota(jnp.int32, (64, 32), 1)
    kept = (position < length_col) & ((position == 0) | (mask_ref[...] == 1))
    valid = jnp.where(kept, 1.0, 0.0).astype(F32)
    valid_own[...] = jnp.concatenate([valid, jnp.zeros((64, 96), F32)], axis=1)
    spread(valid, wide)

    load_x.wait()
    load_slots.wait()

    def gather(d, carry):
        at = d * 64 + p * 2
        first = lax.rem(slots[at], 256)
        second = lax.rem(slots[at + 1], 256)
        both = jnp.concatenate([x[first].astype(F32), x[second].astype(F32)], axis=0)
        scale = lax.rsqrt(jnp.sum(both * both, axis=1, keepdims=True) + 1e-06)
        send[d] = (both * scale).astype(BF16)
        return carry

    lax.fori_loop(0, 128, gather, 0, unroll=8)

    pl.semaphore_wait(barrier, 127)

    def push_own(i, carry):
        te, tz, tx, tc = peer(128 - i)
        tp = tz * 8 + tx * 2 + tc
        pltpu.make_async_remote_copy(
            send.at[te * 32 + tp], tiles_own.at[me], send_own, recv_own, device_id=(te, tp), device_id_type=MESH
        ).start()
        return carry

    def push_next(i, carry):
        te, tz, tx, tc = peer(128 - i)
        tp = tz * 8 + tx * 2 + tc
        unit = te * 32 + tz * 8 + next_x(tx) * 2 + tc
        pltpu.make_async_remote_copy(
            send.at[unit], tiles_next.at[me], send_next, recv_next, device_id=(te, tp), device_id_type=MESH
        ).start()
        return carry

    send_valid = pltpu.make_async_remote_copy(
        valid_own, valid_next, sem_valid.at[0], sem_valid.at[1], device_id=(e, prv), device_id_type=MESH
    )
    send_valid.start()
    pltpu.make_async_copy(send.at[me], tiles_own.at[me], recv_own).start()
    pltpu.make_async_copy(send.at[e * 32 + nxt], tiles_next.at[me], recv_next).start()
    lax.fori_loop(1, 128, push_own, 0)
    lax.fori_loop(1, 128, push_next, 0)

    r = lax.broadcasted_iota(jnp.int32, (128, 128), 0)
    c = lax.broadcasted_iota(jnp.int32, (128, 128), 1)
    move = jnp.where(c == (r % 16) * 8 + r // 16, 1.0, 0.0).astype(F32)
    head = jnp.where(c == (r % 16) * 8, 1.0, 0.0).astype(F32)

    send_valid.wait()
    valid_n = valid_next[...]
    spread(valid_n[:, :32], wide_next)
    turned[...] = valid_n.T[:32, :]
    weight = jnp.concatenate([turned[pl.ds(0, 16, 2), :], turned[pl.ds(1, 16, 2), :]], axis=1)

    pltpu.make_async_copy(tiles_own, tiles_own, recv_own).wait()
    assemble(tiles_own, wide, block, move, head)
    send_block = pltpu.make_async_remote_copy(
        block, block_core, sem_block.at[0], sem_block.at[1], device_id=(e, mate), device_id_type=MESH
    )
    send_block.start()
    send_block.wait()
    forward_only(block, block_core, wide, fore_own)
    send_fore = pltpu.make_async_remote_copy(
        fore_own, fore_core, sem_fore.at[0], sem_fore.at[1], device_id=(e, mate), device_id_type=MESH
    )
    send_fore.start()

    pltpu.make_async_copy(tiles_next, tiles_next, recv_next).wait()
    assemble(tiles_next, wide_next, block_next, move, head)
    both_ways(block, block_next, wide, weight, score)
    score_t[...] = score[...].T[:64, :]
    send_score = pltpu.make_async_remote_copy(
        score_t, score_in, sem_score.at[0], sem_score.at[1], device_id=(e, nxt), device_id_type=MESH
    )
    send_score.start()
    send_fore.wait()
    core_score = 0.5 * (fore_own[:, :64] + fore_core[...].T[:64, :])
    send_score.wait()
    mine = score[:, :64]
    theirs = score_in[...]
    near = jnp.logical_or(xx == 0, xx == 3)
    out_ref[:, 0:64] = core_score
    out_ref[:, 64:128] = jnp.where(near, mine, theirs)
    out_ref[:, 128:192] = jnp.where(near, theirs, mine)
    pltpu.make_async_copy(send.at[pl.ds(0, 127)], send.at[pl.ds(0, 127)], send_own).wait()
    pltpu.make_async_copy(send.at[pl.ds(0, 127)], send.at[pl.ds(0, 127)], send_next).wait()


def shards(encoded, slot_items, lengths, token_mask):
    vmem = pl.BlockSpec(memory_space=pltpu.VMEM)
    hbm = pl.BlockSpec(memory_space=pl.ANY)
    tiles = pltpu.VMEM((128, 16, 128), BF16)
    rows = pltpu.VMEM((32, 64, 128), BF16)
    lanes = pltpu.VMEM((32, 64, 128), F32)
    flat = pltpu.VMEM((64, 128), F32)
    dma = pltpu.SemaphoreType.DMA
    return pl.pallas_call(
        kernel,
        out_shape=jax.ShapeDtypeStruct((64, 192), F32),
        in_specs=[hbm, hbm, vmem, vmem],
        out_specs=vmem,
        scratch_shapes=[
            pltpu.VMEM((256, 8, 128), BF16),
            pltpu.SMEM((8192,), jnp.int32),
            tiles, tiles, tiles, rows, rows, rows,
            flat, flat, pltpu.VMEM((32, 64), F32), lanes, lanes,
            flat, flat, flat, pltpu.VMEM((64, 64), F32), pltpu.VMEM((64, 64), F32),
            dma((2,)), dma, dma, dma, dma, dma((2,)), dma((2,)), dma((2,)), dma((2,)),
        ],
        compiler_params=pltpu.CompilerParams(
            collective_id=0, has_side_effects=True, vmem_limit_bytes=48 * 2**20
        ),
        name="chamfer",
    )(encoded, slot_items, lengths.reshape(1, 64), token_mask)


def solution(mesh):
    in_specs = (P("pool", "enc", None), P(), P(("enc", "pool")), P(("enc", "pool"), None))
    out_specs = P(("enc", "pool"), None)
    return jax.shard_map(shards, mesh=mesh, in_specs=in_specs, out_specs=out_specs, check_vma=False)
```

time: 85.4 us -> 39.7 us (0.46)
  the two profiles are of different devices: /device:TPU:0 before, /device:TPU:1 now
where the time goes in v1:
time: 39.7 us; the launch traced here: 39.4 us
  Pallas kernels  36.9 us (93%)
  local copies, waits for them, and re-layouts  2.48 us (6%)
    pallas_call x1, Pallas kernels, shards(): pl.pallas_call(kernel, out_shape=jax.ShapeDtypeStruct((64, 192), F32), in...  36.9 us
    unnamed x8, local copies, waits for them, and re-layouts  2.48 us

profile of v1, /device:TPU:1, one launch (start us, length us, event | category | flops | bytes accessed | tf_op | source)
XLA Modules:
  0.0 39.4 jit_solution(5839863388622503701)
XLA Ops:
  0.0 0.0 copy-start.1
  0.0 0.0 copy-start.2
  0.0 0.8 %copy.5.mask_ref = s32[64,32]{1,0:T(8,128)S(1)} copy(s32[64,32]{0,1:T(8,128)} %param.7) | data formatting | bytes 16384 | tf_op args[3]
  0.8 0.0 copy-done.1
  0.8 0.0 copy-done.2
  0.8 0.0 copy-start
  0.8 1.0 %copy-done = bf16[256,8,128]{2,1,0:T(8,128)(2,1)S(1)} copy-done((bf16[256,8,128]{2,1,0:T(8,128)(2,1)S(1)}, bf16[256,8,128]{2,1,0:T(8,128)(2,1)}, u32[]{:S(2)}) %copy-start) | copy-done | bytes 524312
  1.9 36.9 %chamfer.1 = f32[64,192]{1,0:T(8,128)S(1)} custom-call(bf16[256,8,128]{2,1,0:T(8,128)(2,1)S(1)} %copy-done, s32[8192]{0:T(1024)S(1)} %copy-done.1, s32[1,64]{1,0:T(1,128)S(1)} %bitcast.1, s32[64,32]{1,0:T(8,128)S(1)} %copy.5.mask_ref), custom_call_target="tpu_custom_call" | custom-call | tf_op jit(solution)/shard_map/chamfer/pallas_call | solution.py:221
  38.8 0.6 %copy.7 = f32[64,192]{1,0:T(8,128)} copy(f32[64,192]{1,0:T(8,128)S(1)} %chamfer.1) | data formatting | bytes 98304
Async XLA Ops:
  0.0 0.8 %copy-start.1 = (s32[8192]{0:T(1024)S(1)}, s32[8192]{0:T(1024)}, u32[]{:S(2)}) copy-start(s32[8192]{0:T(1024)} %slots_hbm.1) | copy-start | bytes 98308
  0.0 0.8 %copy-start.2 = (s32[64]{0:T(128)S(1)}, s32[64]{0:T(128)}, u32[]{:S(2)}) copy-start(s32[64]{0:T(128)} %param.6) | copy-start | bytes 772
  0.8 1.0 %copy-start = (bf16[256,8,128]{2,1,0:T(8,128)(2,1)S(1)}, bf16[256,8,128]{2,1,0:T(8,128)(2,1)}, u32[]{:S(2)}) copy-start(bf16[256,8,128]{2,1,0:T(8,128)(2,1)} %x_hbm.1) | copy-start | bytes 1572868

commit v2 on v1

--- a/solution.py
+++ b/solution.py
@@ -13,6 +13,13 @@
 BF16 = jnp.bfloat16
 
 
+HOP = (0, 1, 2, 1)
+FAR = sorted(
+    [(x, y, z, c) for y in (2, 1, 3, 0) for z in (2, 1, 3, 0) for x in (2, 1, 3, 0) for c in (0, 1)],
+    key=lambda d: -(HOP[d[0]] + HOP[d[1]] + HOP[d[2]]) * 2 - d[3],
+)[:-1]
+
+
 def next_x(x):
     return (2 * x + 1) % 5
 
@@ -21,9 +28,10 @@
     return (3 * x + 2) % 5
 
 
-def spread(valid, wide):
+def spread(turned, wide):
+    valid = jnp.concatenate([turned[...], jnp.zeros((32, 64), F32)], axis=1).T
     for t in range(32):
-        wide[t] = jnp.broadcast_to(valid[:, t : t + 1], (64, 128))
+        wide[t] = jnp.broadcast_to(valid[:64, t : t + 1], (64, 128))
 
 
 def assemble(tiles, wide, out, move, first):
@@ -73,9 +81,9 @@
 
 
 def kernel(
-    x_hbm, slots_hbm, lengths_ref, mask_ref, out_ref,
-    x, slots, send, tiles_own, tiles_next, block, block_next, block_core,
-    valid_own, valid_next, turned, wide, wide_next,
+    x_hbm, slots_hbm, lengths_hbm, mask_hbm, out_ref,
+    x, slots, lengths, mask, send, tiles_own, tiles_next, block, block_next, block_core,
+    valid_own, valid_next, wide, wide_next,
     fore_own, fore_core, score, score_t, score_in,
     load_sem, send_own, send_next, recv_own, recv_next, sem_valid, sem_block, sem_fore, sem_score,
 ):
@@ -91,10 +99,17 @@
 
     load_x = pltpu.make_async_copy(x_hbm, x, load_sem.at[0])
     load_slots = pltpu.make_async_copy(slots_hbm, slots, load_sem.at[1])
-    load_x.start()
-    load_slots.start()
+    load_lengths = pltpu.make_async_copy(lengths_hbm, lengths, load_sem.at[2])
+    load_mask = pltpu.make_async_copy(mask_hbm, mask, load_sem.at[3])
+    loads = (load_x, load_slots, load_lengths, load_mask)
+    for load in loads:
+        load.start()
 
     def peer(i):
+        dx, dy, dz, dc = FAR[i - 1]
+        return (e + dy) % 4, (z + dz) % 4, (xx + dx) % 4, (core + dc) % 2
+
+    def peer_old(i):
         dx = (i // 2) % 4
         dz = (i // 8) % 4
         dy = i // 32
@@ -107,24 +122,15 @@
     barrier = pltpu.get_barrier_semaphore()
 
     def greet(i, carry):
-        te, tz, tx, tc = peer(128 - i)
+        te, tz, tx, tc = peer(i)
         pl.semaphore_signal(barrier, inc=1, device_id=(te, tz * 8 + tx * 2 + tc), device_id_type=MESH)
         return carry
 
-    lax.fori_loop(1, 128, greet, 0)
-
-    length = lengths_ref[...]
-    row = lax.broadcasted_iota(jnp.int32, (64, 64), 0)
-    col = lax.broadcasted_iota(jnp.int32, (64, 64), 1)
-    length_col = jnp.sum(jnp.where(row == col, jnp.broadcast_to(length, (64, 64)), 0), axis=1, keepdims=True)
-    position = lax.broadcasted_iota(jnp.int32, (64, 32), 1)
-    kept = (position < length_col) & ((position == 0) | (mask_ref[...] == 1))
-    valid = jnp.where(kept, 1.0, 0.0).astype(F32)
-    valid_own[...] = jnp.concatenate([valid, jnp.zeros((64, 96), F32)], axis=1)
-    spread(valid, wide)
-
-    load_x.wait()
-    load_slots.wait()
+    for i in range(1, 128):
+        greet(i, 0)
+
+    for load in loads:
+        load.wait()
 
     def gather(d, carry):
         at = d * 64 + p * 2
@@ -137,10 +143,14 @@
 
     lax.fori_loop(0, 128, gather, 0, unroll=8)
 
+    position = lax.broadcasted_iota(jnp.int32, (32, 64), 0)
+    kept = (position < lengths[...]) & ((position == 0) | (mask[...] == 1))
+    valid_own[...] = jnp.where(kept, 1.0, 0.0).astype(F32)
+
     pl.semaphore_wait(barrier, 127)
 
     def push_own(i, carry):
-        te, tz, tx, tc = peer(128 - i)
+        te, tz, tx, tc = peer(i)
         tp = tz * 8 + tx * 2 + tc
         pltpu.make_async_remote_copy(
             send.at[te * 32 + tp], tiles_own.at[me], send_own, recv_own, device_id=(te, tp), device_id_type=MESH
@@ -148,7 +158,7 @@
         return carry
 
     def push_next(i, carry):
-        te, tz, tx, tc = peer(128 - i)
+        te, tz, tx, tc = peer(i)
         tp = tz * 8 + tx * 2 + tc
         unit = te * 32 + tz * 8 + next_x(tx) * 2 + tc
         pltpu.make_async_remote_copy(
@@ -162,19 +172,20 @@
     send_valid.start()
     pltpu.make_async_copy(send.at[me], tiles_own.at[me], recv_own).start()
     pltpu.make_async_copy(send.at[e * 32 + nxt], tiles_next.at[me], recv_next).start()
-    lax.fori_loop(1, 128, push_own, 0)
-    lax.fori_loop(1, 128, push_next, 0)
-
+    for i in range(1, 128):
+        push_own(i, 0)
+    for i in range(1, 128):
+        push_next(i, 0)
+
+    spread(valid_own, wide)
     r = lax.broadcasted_iota(jnp.int32, (128, 128), 0)
     c = lax.broadcasted_iota(jnp.int32, (128, 128), 1)
     move = jnp.where(c == (r % 16) * 8 + r // 16, 1.0, 0.0).astype(F32)
     head = jnp.where(c == (r % 16) * 8, 1.0, 0.0).astype(F32)
 
     send_valid.wait()
-    valid_n = valid_next[...]
-    spread(valid_n[:, :32], wide_next)
-    turned[...] = valid_n.T[:32, :]
-    weight = jnp.concatenate([turned[pl.ds(0, 16, 2), :], turned[pl.ds(1, 16, 2), :]], axis=1)
+    spread(valid_next, wide_next)
+    weight = jnp.concatenate([valid_next[pl.ds(0, 16, 2), :], valid_next[pl.ds(1, 16, 2), :]], axis=1)
 
     pltpu.make_async_copy(tiles_own, tiles_own, recv_own).wait()
     assemble(tiles_own, wide, block, move, head)
@@ -212,7 +223,7 @@
 
 def shards(encoded, slot_items, lengths, token_mask):
     vmem = pl.BlockSpec(memory_space=pltpu.VMEM)
-    hbm = pl.BlockSpec(memory_space=pl.ANY)
+    hbm = pl.BlockSpec(memory_space=pltpu.HBM)
     tiles = pltpu.VMEM((128, 16, 128), BF16)
     rows = pltpu.VMEM((32, 64, 128), BF16)
     lanes = pltpu.VMEM((32, 64, 128), F32)
@@ -221,21 +232,21 @@
     return pl.pallas_call(
         kernel,
         out_shape=jax.ShapeDtypeStruct((64, 192), F32),
-        in_specs=[hbm, hbm, vmem, vmem],
+        in_specs=[hbm] * 4,
         out_specs=vmem,
         scratch_shapes=[
             pltpu.VMEM((256, 8, 128), BF16),
-            pltpu.SMEM((8192,), jnp.int32),
+            pltpu.SMEM((8192,), jnp.int32), pltpu.VMEM((1, 64), jnp.int32), pltpu.VMEM((32, 64), jnp.int32),
             tiles, tiles, tiles, rows, rows, rows,
-            flat, flat, pltpu.VMEM((32, 64), F32), lanes, lanes,
+            pltpu.VMEM((32, 64), F32), pltpu.VMEM((32, 64), F32), lanes, lanes,
             flat, flat, flat, pltpu.VMEM((64, 64), F32), pltpu.VMEM((64, 64), F32),
-            dma((2,)), dma, dma, dma, dma, dma((2,)), dma((2,)), dma((2,)), dma((2,)),
+            dma((4,)), dma, dma, dma, dma, dma((2,)), dma((2,)), dma((2,)), dma((2,)),
         ],
         compiler_params=pltpu.CompilerParams(
-            collective_id=0, has_side_effects=True, vmem_limit_bytes=48 * 2**20
+            collective_id=0, has_side_effects=True, vmem_limit_bytes=61 * 2**20
         ),
         name="chamfer",
-    )(encoded, slot_items, lengths.reshape(1, 64), token_mask)
+    )(encoded, slot_items, lengths.reshape(1, 64), token_mask.T)
 
 
 def solution(mesh):

time: 39.7 us -> 34.2 us (0.86)
  Pallas kernels: 36.9 us -> 32.4 us
  local copies, waits for them, and re-layouts: 2.48 us -> 1.47 us
    pallas_call x1, Pallas kernels: 36.9 us -> 32.4 us  [shards(): pl.pallas_call(kernel, out_shape=jax.ShapeDtypeStruct((64, 192), F32), in...]
    unnamed x8 -> x1, local copies, waits for them, and re-layouts: 2.48 us -> 1.47 us
where the time goes in v2:
time: 34.2 us; the launch traced here: 33.9 us
  Pallas kernels  32.4 us (95%)
  local copies, waits for them, and re-layouts  1.47 us (4%)
    pallas_call x1, Pallas kernels, shards(): pl.pallas_call(kernel, out_shape=jax.ShapeDtypeStruct((64, 192), F32), in...  32.4 us
    unnamed x1, local copies, waits for them, and re-layouts  1.47 us

profile of v2, /device:TPU:1, one launch (start us, length us, event | category | flops | bytes accessed | tf_op | source)
XLA Modules:
  0.0 33.9 jit_solution(8520020577187478684)
XLA Ops:
  0.0 32.4 %chamfer.1 = f32[64,192]{1,0:T(8,128)} custom-call(bf16[256,8,128]{2,1,0:T(8,128)(2,1)} %x_hbm.1, s32[8192]{0:T(1024)} %slots_hbm.1, s32[1,64]{1,0:T(1,128)} %bitcast.3, s32[32,64]{1,0:T(8,128)} %bitcast.2), custom_call_target="tpu_custom_call" | custom-call | tf_op jit(solution)/shard_map/chamfer/pallas_call | solution.py:232
  32.4 1.5 %copy.6 = f32[64,192]{1,0:T(8,128)} copy(f32[64,192]{1,0:T(8,128)} %chamfer.1) | data formatting | bytes 98304

commit v3 on v2

v3 whole, which is shorter than its diff:
```python
import functools

import jax
import jax.numpy as jnp
from jax import lax
from jax.experimental import pallas as pl
from jax.experimental.pallas import tpu as pltpu
from jax.sharding import PartitionSpec as P

MESH = pl.DeviceIdType.MESH
NT = (((1,), (1,)), ((), ()))
F32 = jnp.float32
BF16 = jnp.bfloat16


HOP = (0, 1, 2, 1)
CHUNK = 127
FAR = sorted(
    [(x, y, z, c) for y in (2, 1, 3, 0) for z in (2, 1, 3, 0) for x in (2, 1, 3, 0) for c in (0, 1)],
    key=lambda d: -(HOP[d[0]] + HOP[d[1]] + HOP[d[2]]) * 2 - d[3],
)[:-1]


def next_x(x):
    return (2 * x + 1) % 5


def prev_x(x):
    return (3 * x + 2) % 5


def spread(turned, wide):
    valid = jnp.concatenate([turned[...], jnp.zeros((32, 64), F32)], axis=1).T
    for t in range(32):
        column = jnp.broadcast_to(valid[:64, t : t + 1], (64, 128))
        for at in range(4):
            wide[at, t] = column[at * 16 : at * 16 + 16]


def group_rows(rank):
    return pl.ds(pl.multiple_of(rank * 8, 8), 8)


def assemble(tiles, wide, out, move, head, rank):
    at = rank // 4
    y = rank % 4
    tokens = pl.ds(pl.multiple_of(y * 8, 8), 8)
    rows = tiles[group_rows(rank)].reshape(128, 128)
    base = tiles[group_rows(at * 4)].reshape(128, 128)
    keep = wide[at, tokens].reshape(128, 128)
    take = jnp.concatenate([keep * move, (1.0 - keep) * head], axis=1).astype(BF16)
    both = jnp.concatenate([rows, base], axis=0)
    made = jnp.dot(take, both, preferred_element_type=F32).astype(BF16)
    out[at, tokens] = made.reshape(8, 16, 128)


def columns(block, n):
    return jnp.concatenate([block[at, u] for u in range(4 * n, 4 * n + 4) for at in range(4)], axis=0)


def fore_sum(fore, wide, a):
    best = jnp.maximum(fore, pltpu.roll(fore, 64, 1)).reshape(32, 16, 128)
    return jnp.sum(best * wide[a], axis=0)


def quarter(block, other, wide, weight, rows, cols, out):
    for i in range(2):
        a = 2 * rows + i
        left = block[a].reshape(512, 128)
        fore = None
        back = None
        for n in range(4):
            right = jnp.concatenate(
                [other[2 * cols + h, u] for u in range(8 * n, 8 * n + 8) for h in range(2)], axis=0
            )
            dots = lax.dot_general(left, right, NT, preferred_element_type=F32)
            part = jnp.maximum(dots[:, :128], dots[:, 128:])
            fore = part if fore is None else jnp.maximum(fore, part)
            most = jnp.max(dots.reshape(32, 16, 256), axis=0)
            part = most[:, :128] * weight[2 * n : 2 * n + 1, :] + most[:, 128:] * weight[2 * n + 1 : 2 * n + 2, :]
            back = part if back is None else back + part
        back = back + pltpu.roll(back, 64, 1)
        back = back + pltpu.roll(back, 32, 1)
        fore = jnp.maximum(fore, pltpu.roll(fore, 64, 1))
        fore = jnp.maximum(fore, pltpu.roll(fore, 32, 1)).reshape(32, 16, 128)
        out[i * 16 : i * 16 + 16, :] = 0.5 * (jnp.sum(fore * wide[a], axis=0) + back)


def both_ways(block, other, wide, weight, out):
    for a in range(4):
        left = block[a].reshape(512, 128)
        fore = None
        back = None
        for n in range(8):
            right = columns(other, n)
            dots = lax.dot_general(left, right, NT, preferred_element_type=F32)
            part = jnp.maximum(dots[:, :128], dots[:, 128:])
            fore = part if fore is None else jnp.maximum(fore, part)
            most = jnp.max(dots.reshape(32, 16, 256), axis=0)
            part = most[:, :128] * weight[2 * n : 2 * n + 1, :] + most[:, 128:] * weight[2 * n + 1 : 2 * n + 2, :]
            back = part if back is None else back + part
        back = back + pltpu.roll(back, 64, 1)
        out[a * 16 : a * 16 + 16, :] = 0.5 * (fore_sum(fore, wide, a) + back)


def kernel(
    x_hbm, slots_hbm, lengths_hbm, mask_hbm, out_ref,
    x, slots, lengths, mask, send, tiles_own, tiles_next, block, block_next, block_core,
    valid_own, valid_next, valid_core, wide, wide_next,
    part_own, part_in, score, score_t, score_in,
    load_sem, send_own, send_next, recv_own, recv_next, sem_valid, sem_out, sem_in, sem_fore, sem_score,
):
    e = lax.axis_index("enc")
    p = lax.axis_index("pool")
    z = p // 8
    xx = (p // 2) % 4
    core = p % 2
    me = e * 32 + p
    nxt = z * 8 + next_x(xx) * 2 + core
    prv = z * 8 + prev_x(xx) * 2 + core
    mate = z * 8 + xx * 2 + (1 - core)

    load_x = pltpu.make_async_copy(x_hbm, x, load_sem.at[0])
    load_slots = pltpu.make_async_copy(slots_hbm, slots, load_sem.at[1])
    load_lengths = pltpu.make_async_copy(lengths_hbm, lengths, load_sem.at[2])
    load_mask = pltpu.make_async_copy(mask_hbm, mask, load_sem.at[3])
    loads = (load_x, load_slots, load_lengths, load_mask)
    for load in loads:
        load.start()

    rank = z * 4 + e
    slot = rank * 8 + xx * 2 + core
    def peer(i):
        dx, dy, dz, dc = FAR[i]
        return (e + dy) % 4, (z + dz) % 4, (xx + dx) % 4, (core + dc) % 2

    barrier = pltpu.get_barrier_semaphore()
    for i in range(127):
        te, tz, tx, tc = peer(i)
        pl.semaphore_signal(barrier, inc=1, device_id=(te, tz * 8 + tx * 2 + tc), device_id_type=MESH)

    for load in loads:
        load.wait()

    def gather(d):
        at = d * 64 + p * 2
        first = lax.rem(slots[at], 256)
        second = lax.rem(slots[at + 1], 256)
        both = jnp.concatenate([x[first].astype(F32), x[second].astype(F32)], axis=0)
        scale = lax.rsqrt(jnp.sum(both * both, axis=1, keepdims=True) + 1e-06)
        send[d] = (both * scale).astype(BF16)

    def push(which, part):
        for i in part:
            te, tz, tx, tc = peer(i)
            if which == 0:
                unit = te * 32 + tz * 8 + tx * 2 + tc
                tiles, sent, got = tiles_own, send_own, recv_own
            else:
                unit = te * 32 + tz * 8 + next_x(tx) * 2 + tc
                tiles, sent, got = tiles_next, send_next, recv_next
            pltpu.make_async_remote_copy(
                send.at[unit], tiles.at[slot], sent, got.at[rank], device_id=(te, tz * 8 + tx * 2 + tc), device_id_type=MESH
            ).start()

    def arrived(tiles, got, k):
        rows = tiles.at[group_rows(k)]
        pltpu.make_async_copy(rows, rows, got.at[k]).wait()

    position = lax.broadcasted_iota(jnp.int32, (32, 64), 0)
    kept = (position < lengths[...]) & ((position == 0) | (mask[...] == 1))
    valid_own[...] = jnp.where(kept, 1.0, 0.0).astype(F32)

    def valid_copy(i, to):
        there = (valid_next, valid_core)[i]
        return pltpu.make_async_remote_copy(
            valid_own, there, sem_valid.at[2 * i], sem_valid.at[2 * i + 1], device_id=(e, to), device_id_type=MESH
        )

    send_valid = (valid_copy(0, prv), valid_copy(1, mate))

    for first in range(0, 127, CHUNK):
        part = range(first, min(first + CHUNK, 127))
        for i in part:
            te, tz, tx, tc = peer(i)
            gather(te * 32 + tz * 8 + tx * 2 + tc)
        if first == 0:
            pl.semaphore_wait(barrier, 127)
            for copy in send_valid:
                copy.start()
        push(0, part)
    gather(me)
    pltpu.make_async_copy(send.at[me], tiles_own.at[slot], recv_own.at[rank]).start()
    pltpu.make_async_copy(send.at[e * 32 + nxt], tiles_next.at[slot], recv_next.at[rank]).start()
    push(1, range(127))

    spread(valid_own, wide)
    r = lax.broadcasted_iota(jnp.int32, (128, 128), 0)
    c = lax.broadcasted_iota(jnp.int32, (128, 128), 1)
    move = jnp.where(c == (r % 16) * 8 + r // 16, 1.0, 0.0).astype(F32)
    head = jnp.where(c == (r % 16) * 8, 1.0, 0.0).astype(F32)

    for copy in send_valid:
        copy.wait()
    spread(valid_next, wide_next)
    weight = jnp.concatenate([valid_next[pl.ds(0, 16, 2), :], valid_next[pl.ds(1, 16, 2), :]], axis=1)
    weights_core = [
        jnp.concatenate([valid_core[pl.ds(k, 8, 4), :][:, h * 32 : h * 32 + 32] for k in range(4)], axis=1) for h in range(2)
    ]

    def core_copy(at):
        return pltpu.make_async_remote_copy(
            block.at[at], block_core.at[at], sem_out.at[at], sem_in.at[at],
            device_id=(e, mate), device_id_type=MESH,
        )

    for dz in (2, 1, 3, 0):
        at = (z + dz) % 4
        for y in range(4):
            arrived(tiles_own, recv_own, at * 4 + y)
        for y in range(4):
            assemble(tiles_own, wide, block, move, head, at * 4 + y)
        core_copy(at).start()
    for dz in (2, 1, 3, 0):
        at = (z + dz) % 4
        for y in range(4):
            arrived(tiles_next, recv_next, at * 4 + y)
        for y in range(4):
            assemble(tiles_next, wide_next, block_next, move, head, at * 4 + y)
    both_ways(block, block_next, wide, weight, score)
    score_t[...] = score[...].T[:64, :]
    send_score = pltpu.make_async_remote_copy(
        score_t, score_in, sem_score.at[0], sem_score.at[1], device_id=(e, nxt), device_id_type=MESH
    )
    send_score.start()
    for at in range(4):
        core_copy(at).wait()
    quarter_copies = []
    for j in range(2):
        rows = j * (1 - core) + core
        cols = j * core
        weight_core = jnp.where(cols == 0, weights_core[0], weights_core[1])
        quarter(block, block_core, wide, weight_core, rows, cols, part_own.at[j])
        copy = pltpu.make_async_remote_copy(
            part_own.at[j], part_in.at[j], sem_fore.at[2 * j], sem_fore.at[2 * j + 1],
            device_id=(e, mate), device_id_type=MESH,
        )
        copy.start()
        quarter_copies.append(copy)
    send_score.wait()
    mine = score[:, :64]
    theirs = score_in[...]
    near = jnp.logical_or(xx == 0, xx == 3)
    out_ref[:, 64:128] = jnp.where(near, mine, theirs)
    out_ref[:, 128:192] = jnp.where(near, theirs, mine)
    for copy in quarter_copies:
        copy.wait()
    q0, q1 = (part_own[j][:, :32] for j in range(2))
    r0, r1 = (part_in[j].T[:32, :] for j in range(2))
    out_ref[0:32, 0:32] = jnp.where(core == 0, q0, r0)
    out_ref[0:32, 32:64] = jnp.where(core == 0, r0, r1)
    out_ref[32:64, 0:32] = jnp.where(core == 0, q1, q0)
    out_ref[32:64, 32:64] = jnp.where(core == 0, r1, q1)
    pltpu.make_async_copy(send.at[pl.ds(0, 127)], send.at[pl.ds(0, 127)], send_own).wait()
    pltpu.make_async_copy(send.at[pl.ds(0, 127)], send.at[pl.ds(0, 127)], send_next).wait()


def shards(encoded, slot_items, lengths, token_mask):
    vmem = pl.BlockSpec(memory_space=pltpu.VMEM)
    hbm = pl.BlockSpec(memory_space=pltpu.HBM)
    tiles = pltpu.VMEM((128, 16, 128), BF16)
    rows = pltpu.VMEM((4, 32, 16, 128), BF16)
    lanes = pltpu.VMEM((4, 32, 16, 128), F32)
    flat = pltpu.VMEM((64, 128), F32)
    dma = pltpu.SemaphoreType.DMA
    return pl.pallas_call(
        kernel,
        out_shape=jax.ShapeDtypeStruct((64, 192), F32),
        in_specs=[hbm] * 4,
        out_specs=vmem,
        scratch_shapes=[
            pltpu.VMEM((256, 8, 128), BF16),
            pltpu.SMEM((8192,), jnp.int32), pltpu.VMEM((1, 64), jnp.int32), pltpu.VMEM((32, 64), jnp.int32),
            tiles, tiles, tiles, rows, rows, rows,
            pltpu.VMEM((32, 64), F32), pltpu.VMEM((32, 64), F32), pltpu.VMEM((32, 64), F32), lanes, lanes,
            pltpu.VMEM((2, 32, 128), F32), pltpu.VMEM((2, 32, 128), F32), flat, pltpu.VMEM((64, 64), F32), pltpu.VMEM((64, 64), F32),
            dma((4,)), dma, dma, dma((16,)), dma((16,)), dma((4,)), dma((4,)), dma((4,)),
            dma((4,)), dma((2,)),
        ],
        compiler_params=pltpu.CompilerParams(
            collective_id=0, has_side_effects=True, vmem_limit_bytes=61 * 2**20
        ),
        name="chamfer",
    )(encoded, slot_items, lengths.reshape(1, 64), token_mask.T)


def solution(mesh):
    in_specs = (P("pool", "enc", None), P(), P(("enc", "pool")), P(("enc", "pool"), None))
    out_specs = P(("enc", "pool"), None)
    return jax.shard_map(shards, mesh=mesh, in_specs=in_specs, out_specs=out_specs, check_vma=False)
```

time: 34.2 us -> 33.5 us (0.980)
  Pallas kernels: 32.4 us -> 31.8 us
    pallas_call x1, Pallas kernels: 32.4 us -> 31.8 us  [shards(): pl.pallas_call(kernel, out_shape=jax.ShapeDtypeStruct((64, 192), F32), in...]
where the time goes in v3:
time: 33.5 us; the launch traced here: 33.3 us
  Pallas kernels  31.8 us (95%)
  local copies, waits for them, and re-layouts  1.47 us (4%)
    pallas_call x1, Pallas kernels, shards(): pl.pallas_call(kernel, out_shape=jax.ShapeDtypeStruct((64, 192), F32), in...  31.8 us
    unnamed x1, local copies, waits for them, and re-layouts  1.47 us

profile of v3, /device:TPU:1, one launch (start us, length us, event | category | flops | bytes accessed | tf_op | source)
XLA Modules:
  0.0 33.3 jit_solution(15499528816414133107)
XLA Ops:
  0.0 31.8 %chamfer.1 = f32[64,192]{1,0:T(8,128)} custom-call(bf16[256,8,128]{2,1,0:T(8,128)(2,1)} %x_hbm.1, s32[8192]{0:T(1024)} %slots_hbm.1, s32[1,64]{1,0:T(1,128)} %bitcast.3, s32[32,64]{1,0:T(8,128)} %bitcast.2), custom_call_target="tpu_custom_call" | custom-call | tf_op jit(solution)/shard_map/chamfer/pallas_call | solution.py:276
  31.8 1.5 %copy.6 = f32[64,192]{1,0:T(8,128)} copy(f32[64,192]{1,0:T(8,128)} %chamfer.1) | data formatting | bytes 98304

commit v4 on v3

--- a/solution.py
+++ b/solution.py
@@ -61,29 +61,6 @@
 def fore_sum(fore, wide, a):
     best = jnp.maximum(fore, pltpu.roll(fore, 64, 1)).reshape(32, 16, 128)
     return jnp.sum(best * wide[a], axis=0)
-
-
-def quarter(block, other, wide, weight, rows, cols, out):
-    for i in range(2):
-        a = 2 * rows + i
-        left = block[a].reshape(512, 128)
-        fore = None
-        back = None
-        for n in range(4):
-            right = jnp.concatenate(
-                [other[2 * cols + h, u] for u in range(8 * n, 8 * n + 8) for h in range(2)], axis=0
-            )
-            dots = lax.dot_general(left, right, NT, preferred_element_type=F32)
-            part = jnp.maximum(dots[:, :128], dots[:, 128:])
-            fore = part if fore is None else jnp.maximum(fore, part)
-            most = jnp.max(dots.reshape(32, 16, 256), axis=0)
-            part = most[:, :128] * weight[2 * n : 2 * n + 1, :] + most[:, 128:] * weight[2 * n + 1 : 2 * n + 2, :]
-            back = part if back is None else back + part
-        back = back + pltpu.roll(back, 64, 1)
-        back = back + pltpu.roll(back, 32, 1)
-        fore = jnp.maximum(fore, pltpu.roll(fore, 64, 1))
-        fore = jnp.maximum(fore, pltpu.roll(fore, 32, 1)).reshape(32, 16, 128)
-        out[i * 16 : i * 16 + 16, :] = 0.5 * (jnp.sum(fore * wide[a], axis=0) + back)
 
 
 def both_ways(block, other, wide, weight, out):
@@ -107,8 +84,8 @@
     x_hbm, slots_hbm, lengths_hbm, mask_hbm, out_ref,
     x, slots, lengths, mask, send, tiles_own, tiles_next, block, block_next, block_core,
     valid_own, valid_next, valid_core, wide, wide_next,
-    part_own, part_in, score, score_t, score_in,
-    load_sem, send_own, send_next, recv_own, recv_next, sem_valid, sem_out, sem_in, sem_fore, sem_score,
+    score_core, score, score_t, score_in,
+    load_sem, send_own, send_next, recv_own, recv_next, sem_valid, sem_out, sem_in, sem_score,
 ):
     e = lax.axis_index("enc")
     p = lax.axis_index("pool")
@@ -204,9 +181,7 @@
         copy.wait()
     spread(valid_next, wide_next)
     weight = jnp.concatenate([valid_next[pl.ds(0, 16, 2), :], valid_next[pl.ds(1, 16, 2), :]], axis=1)
-    weights_core = [
-        jnp.concatenate([valid_core[pl.ds(k, 8, 4), :][:, h * 32 : h * 32 + 32] for k in range(4)], axis=1) for h in range(2)
-    ]
+    weight_core = jnp.concatenate([valid_core[pl.ds(0, 16, 2), :], valid_core[pl.ds(1, 16, 2), :]], axis=1)
 
     def core_copy(at):
         return pltpu.make_async_remote_copy(
@@ -235,32 +210,14 @@
     send_score.start()
     for at in range(4):
         core_copy(at).wait()
-    quarter_copies = []
-    for j in range(2):
-        rows = j * (1 - core) + core
-        cols = j * core
-        weight_core = jnp.where(cols == 0, weights_core[0], weights_core[1])
-        quarter(block, block_core, wide, weight_core, rows, cols, part_own.at[j])
-        copy = pltpu.make_async_remote_copy(
-            part_own.at[j], part_in.at[j], sem_fore.at[2 * j], sem_fore.at[2 * j + 1],
-            device_id=(e, mate), device_id_type=MESH,
-        )
-        copy.start()
-        quarter_copies.append(copy)
+    both_ways(block, block_core, wide, weight_core, score_core)
+    out_ref[:, 0:64] = score_core[:, :64]
     send_score.wait()
     mine = score[:, :64]
     theirs = score_in[...]
     near = jnp.logical_or(xx == 0, xx == 3)
     out_ref[:, 64:128] = jnp.where(near, mine, theirs)
     out_ref[:, 128:192] = jnp.where(near, theirs, mine)
-    for copy in quarter_copies:
-        copy.wait()
-    q0, q1 = (part_own[j][:, :32] for j in range(2))
-    r0, r1 = (part_in[j].T[:32, :] for j in range(2))
-    out_ref[0:32, 0:32] = jnp.where(core == 0, q0, r0)
-    out_ref[0:32, 32:64] = jnp.where(core == 0, r0, r1)
-    out_ref[32:64, 0:32] = jnp.where(core == 0, q1, q0)
-    out_ref[32:64, 32:64] = jnp.where(core == 0, r1, q1)
     pltpu.make_async_copy(send.at[pl.ds(0, 127)], send.at[pl.ds(0, 127)], send_own).wait()
     pltpu.make_async_copy(send.at[pl.ds(0, 127)], send.at[pl.ds(0, 127)], send_next).wait()
 
@@ -283,9 +240,9 @@
             pltpu.SMEM((8192,), jnp.int32), pltpu.VMEM((1, 64), jnp.int32), pltpu.VMEM((32, 64), jnp.int32),
             tiles, tiles, tiles, rows, rows, rows,
             pltpu.VMEM((32, 64), F32), pltpu.VMEM((32, 64), F32), pltpu.VMEM((32, 64), F32), lanes, lanes,
-            pltpu.VMEM((2, 32, 128), F32), pltpu.VMEM((2, 32, 128), F32), flat, pltpu.VMEM((64, 64), F32), pltpu.VMEM((64, 64), F32),
+            flat, flat, pltpu.VMEM((64, 64), F32), pltpu.VMEM((64, 64), F32),
             dma((4,)), dma, dma, dma((16,)), dma((16,)), dma((4,)), dma((4,)), dma((4,)),
-            dma((4,)), dma((2,)),
+            dma((2,)),
         ],
         compiler_params=pltpu.CompilerParams(
             collective_id=0, has_side_effects=True, vmem_limit_bytes=61 * 2**20

time: 33.5 us -> 33 us (0.985)
  Pallas kernels: 31.8 us -> 31 us
    pallas_call x1, Pallas kernels: 31.8 us -> 31 us  [shards(): pl.pallas_call(kernel, out_shape=jax.ShapeDtypeStruct((64, 192), F32), in...]
where the time goes in v4:
time: 33 us; the launch traced here: 32.5 us
  Pallas kernels  31 us (94%)
  local copies, waits for them, and re-layouts  1.47 us (4%)
    pallas_call x1, Pallas kernels, shards(): pl.pallas_call(kernel, out_shape=jax.ShapeDtypeStruct((64, 192), F32), in...  31 us
    unnamed x1, local copies, waits for them, and re-layouts  1.47 us

profile of v4, /device:TPU:1, one launch (start us, length us, event | category | flops | bytes accessed | tf_op | source)
XLA Modules:
  0.0 32.5 jit_solution(15956177895222558392)
XLA Ops:
  0.0 31.0 %chamfer.1 = f32[64,192]{1,0:T(8,128)} custom-call(bf16[256,8,128]{2,1,0:T(8,128)(2,1)} %x_hbm.1, s32[8192]{0:T(1024)} %slots_hbm.1, s32[1,64]{1,0:T(1,128)} %bitcast.3, s32[32,64]{1,0:T(8,128)} %bitcast.2), custom_call_target="tpu_custom_call" | custom-call | tf_op jit(solution)/shard_map/chamfer/pallas_call | solution.py:233
  31.0 1.5 %copy.6 = f32[64,192]{1,0:T(8,128)} copy(f32[64,192]{1,0:T(8,128)} %chamfer.1) | data formatting | bytes 98304
